TPU v7x, 128 devices: a whole 4x4x4 slice. The times are simulated.
128 devices in a mesh: grp: 4 (over x), fsdp: 32 (over y, z, core).
Axes of the slice: x: 4, y: 4, z: 4, core: 2. Of those that a mesh axis runs over, the one named last changes fastest.
Arguments:
- tokens: bfloat16 [8192, 4096], P('fsdp'), may hold values from -550 to 550
- attn_gain: float32 [4096], replicated, may hold values from 0.1 to 1.9
- ffn_gain: float32 [4096], replicated, may hold values from 0.1 to 1.9
- w_query: bfloat16 [4096, 4096], P('fsdp', 'grp'), may hold values from -2.421875 to 2.421875
- w_key: bfloat16 [4096, 256], P('fsdp'), may hold values from -0.078125 to 0.078125
- value_weight: bfloat16 [4096, 256], P('fsdp'), may hold values from -0.09375 to 0.09375
- w_out: bfloat16 [4096, 4096], P('grp', 'fsdp'), may hold values from -0.5 to 0.5
- routes: int32 [8192, 8], P('fsdp'), may hold values from 0 to 127, all different within a row; in each aligned block of 256 rows (0 to 255, 256 to 511, ...) at most 24 rows name the same one
- route_probs: bfloat16 [8192, 8], P('fsdp'), may hold values from 0.049804688 to 0.3984375
- w_gate_up: bfloat16 [128, 4096, 1536], P(('grp', 'fsdp')), may hold values from -0.09375 to 0.09375
- w_down: bfloat16 [128, 768, 4096], P(('grp', 'fsdp')), may hold values from -0.21875 to 0.21875
Outputs:
- attn_branch: bfloat16 [8192, 4096], P('fsdp')
- layer_out: bfloat16 [8192, 4096], P('fsdp', 'grp')
Inputs may be any that keep to these rules, and one draw needn't show every extreme that they name: `routes`: each row names 8 different experts. Among the 256 rows of one device (aligned blocks), no expert is named more than 24 times, a bound that some block reaches.
All inputs are finite; a program needn't handle non-finite values.
Results may differ from a plain program's by a relative error of at most 0.015.
Values may be sent and summed in bfloat16 or wider, within the bound.
No kernel may reach another device: no remote copies, remote signals or barrier semaphores. Data moves between devices by JAX's collectives and lax.ppermute only.
A program may use at most 128 MiB of HBM per device.

v0:
```python
import jax
import jax.numpy as jnp
from jax import lax
from jax.sharding import PartitionSpec as P

KEY_VALUE_HEADS = 2
HEAD_DIMENSION = 128
FFW = 768
EPSILON = 1e-06
FLOOR_SCORE = -1e30


def rms_scale(row_data, gain):
    floats = row_data.astype(jnp.float32)
    mean_sq = jnp.mean(floats * floats, axis=-1, keepdims=True)
    return (floats * lax.rsqrt(mean_sq + EPSILON) * gain).astype(jnp.bfloat16)


def attend_block(state, query_bf, key_block, value_block, key_start, positions):
    row_best, row_total, weighted = state
    scores = jnp.einsum(
        "thd,kd->thk", query_bf, key_block, preferred_element_type=jnp.float32
    ) * HEAD_DIMENSION ** (-0.5)
    key_pos = key_start + jnp.arange(key_block.shape[0], dtype=jnp.int32)
    allowed = (key_pos[None, :] <= positions[:, None])[:, None, :]
    masked = jnp.where(allowed, scores, FLOOR_SCORE)
    new_best = jnp.maximum(row_best, jnp.max(masked, axis=2))
    weights = jnp.where(allowed, jnp.exp(masked - new_best[:, :, None]), 0.0)
    rescale = jnp.exp(row_best - new_best)
    row_total = row_total * rescale + jnp.sum(weights, axis=2)
    weighted = weighted * rescale[:, :, None] + jnp.einsum(
        "thk,kd->thd", weights.astype(jnp.bfloat16), value_block, preferred_element_type=jnp.float32
    )
    return (new_best, row_total, weighted)


def on_device(
    tokens,
    attn_gain,
    ffn_gain,
    w_query,
    w_key,
    value_weight,
    w_out,
    routes,
    route_probs,
    w_gate_up,
    w_down,
):
    head_groups = lax.axis_size("grp")
    fsdp_size = lax.axis_size("fsdp")
    current_group = lax.axis_index("grp")
    my_rank = lax.axis_index("fsdp")
    tok_rows = tokens.shape[0]
    model_width = tokens.shape[1]
    head_width = w_query.shape[1]
    group_heads = head_width // HEAD_DIMENSION
    key_value_head = current_group * KEY_VALUE_HEADS // head_groups
    normed = rms_scale(tokens, attn_gain)
    key_cols = lax.dynamic_slice_in_dim(w_key, key_value_head * HEAD_DIMENSION, HEAD_DIMENSION, 1)
    value_cols = lax.dynamic_slice_in_dim(
        value_weight, key_value_head * HEAD_DIMENSION, HEAD_DIMENSION, 1
    )
    query = jnp.dot(
        normed,
        lax.all_gather(w_query, "fsdp", axis=0, tiled=True),
        preferred_element_type=jnp.float32,
    )
    key_local = jnp.dot(
        normed,
        lax.all_gather(key_cols, "fsdp", axis=0, tiled=True),
        preferred_element_type=jnp.float32,
    )
    value_local = jnp.dot(
        normed,
        lax.all_gather(value_cols, "fsdp", axis=0, tiled=True),
        preferred_element_type=jnp.float32,
    )
    query_bf = query.astype(jnp.bfloat16).reshape(tok_rows, group_heads, HEAD_DIMENSION)
    key_local = key_local.astype(jnp.bfloat16)
    value_local = value_local.astype(jnp.bfloat16)
    first_row = my_rank * tok_rows
    positions = first_row + jnp.arange(tok_rows, dtype=jnp.int32)
    last_query = first_row + tok_rows - 1
    attend_init = (
        jnp.full((tok_rows, group_heads), FLOOR_SCORE, jnp.float32),
        jnp.zeros((tok_rows, group_heads), jnp.float32),
        jnp.zeros((tok_rows, group_heads, HEAD_DIMENSION), jnp.float32),
    )
    state = attend_init
    key_rows = lax.all_gather(key_local, "fsdp", axis=0, tiled=True)
    value_rows = lax.all_gather(value_local, "fsdp", axis=0, tiled=True)
    row_count = key_rows.shape[0]
    key_span = 1024

    def visit(running, step_index):
        block_start = step_index * key_span
        key_block = lax.dynamic_slice_in_dim(key_rows, block_start, key_span, 0)
        value_block = lax.dynamic_slice_in_dim(value_rows, block_start, key_span, 0)
        needed = block_start <= last_query
        running = lax.cond(
            needed,
            lambda inner: attend_block(
                inner, query_bf, key_block, value_block, block_start, positions
            ),
            lambda inner: inner,
            running,
        )
        return (running, None)

    state, _ = lax.scan(visit, state, jnp.arange(row_count // key_span, dtype=jnp.int32))
    row_best, row_total, weighted = state
    attended = (weighted / row_total[:, :, None]).astype(jnp.bfloat16).reshape(tok_rows, head_width)
    head_part = jnp.dot(
        attended,
        lax.all_gather(w_out, "fsdp", axis=1, tiled=True),
        preferred_element_type=jnp.float32,
    ).astype(jnp.bfloat16)
    attn_branch = lax.psum(head_part.astype(jnp.float32).astype(jnp.bfloat16), "grp")
    resid = (tokens.astype(jnp.float32) + attn_branch.astype(jnp.float32)).astype(jnp.bfloat16)
    ffn_in = rms_scale(resid, ffn_gain)
    top_count = routes.shape[1]
    experts_all = head_groups * fsdp_size
    capacity = max(2, 3 * tok_rows * top_count // (2 * experts_all))
    group_rows = fsdp_size * capacity
    group_experts = fsdp_size
    expert_ids = current_group * group_experts + jnp.arange(group_experts, dtype=jnp.int32)
    named = routes[:, :, None] == expert_ids[None, None, :]
    hits = jnp.any(named, axis=1)
    token_ids = jnp.arange(tok_rows, dtype=jnp.int32)
    earlier = (token_ids[None, :] < token_ids[:, None]).astype(jnp.bfloat16)
    rank = jnp.dot(earlier, hits.astype(jnp.bfloat16), preferred_element_type=jnp.float32)
    code = jnp.where(hits, rank, -1.0).astype(jnp.bfloat16)
    row_ids = jnp.arange(group_rows, dtype=jnp.int32)
    spread = (
        row_ids[None, :] // capacity == jnp.arange(group_experts, dtype=jnp.int32)[:, None]
    ).astype(jnp.bfloat16)
    code_rows = jnp.dot(code, spread, preferred_element_type=jnp.float32)
    slot_match = code_rows == (row_ids % capacity).astype(jnp.float32)[None, :]
    chosen = slot_match.astype(jnp.bfloat16)
    outbound = (
        jnp.einsum("tr,td->rd", chosen, ffn_in, preferred_element_type=jnp.float32)
        .astype(jnp.bfloat16)
        .reshape(fsdp_size, capacity, model_width)
    )
    gate_proj = w_gate_up[0]
    down_proj = w_down[0]
    col_width = model_width // head_groups
    arrived = lax.all_to_all(outbound, "fsdp", split_axis=0, concat_axis=0, tiled=True)
    slot_count = arrived.shape[1]
    arrived_rows = arrived.reshape(-1, model_width)
    gate_up = jnp.dot(arrived_rows, gate_proj, preferred_element_type=jnp.float32)
    hidden = (jax.nn.silu(gate_up[:, :FFW]) * gate_up[:, FFW:]).astype(jnp.bfloat16)
    result = jnp.dot(hidden, down_proj, preferred_element_type=jnp.float32).astype(jnp.bfloat16)
    returned = lax.all_to_all(
        result.reshape(fsdp_size, slot_count, model_width),
        "fsdp",
        split_axis=0,
        concat_axis=0,
        tiled=True,
    )
    named_probs = jnp.sum(jnp.where(named, route_probs[:, :, None], 0.0), axis=1)
    prob_rows = jnp.dot(
        named_probs.astype(jnp.bfloat16), spread, preferred_element_type=jnp.float32
    )
    mixing = jnp.where(slot_match, prob_rows, 0.0).astype(jnp.bfloat16)
    group_part = jnp.dot(
        mixing, returned.reshape(group_rows, model_width), preferred_element_type=jnp.float32
    ).astype(jnp.bfloat16)
    expert_mix = lax.psum_scatter(
        group_part.astype(jnp.float32).astype(jnp.bfloat16), "grp", scatter_dimension=1, tiled=True
    ).astype(jnp.float32)
    own_cols = lax.dynamic_slice_in_dim(resid, current_group * col_width, col_width, 1)
    layer_out = (own_cols.astype(jnp.float32) + expert_mix).astype(jnp.bfloat16)
    return (attn_branch, layer_out)


def solution(mesh):
    placed = (
        P("fsdp", None),
        P(),
        P(),
        P("fsdp", "grp"),
        P("fsdp", None),
        P("fsdp", None),
        P("grp", "fsdp"),
        P("fsdp", None),
        P("fsdp", None),
        P(("grp", "fsdp"), None, None),
        P(("grp", "fsdp"), None, None),
    )
    return jax.shard_map(
        on_device,
        mesh=mesh,
        in_specs=placed,
        out_specs=(P("fsdp", None), P("fsdp", "grp")),
        check_vma=False,
    )
```

profile of v0, /device:TPU:1, one launch (start us, length us, event | category | flops | bytes accessed | tf_op | source)
XLA Modules:
  0.0 637.6 jit_solution(7689715145708267044)
XLA Ops:
  13.0 44.5 %all-gather.13.cloned.1.call-done = bf16[4096,128]{1,0:T(8,128)(2,1)} async-done(((bf16[128,128]{1,0:T(8,128)(2,1)}), bf16[4096,128]{1,0:T(8,128)(2,1)}) %all-gather.13.cloned.1.call-update) | async-done | bytes 1048592 | tf_op jit(solution)/shard_map/all_gather | solution.py:76
  57.5 3.3 convolution_convert_fusion.5
  60.9 41.6 %all-gather.7.cloned.1.call-done = bf16[4096,128]{1,0:T(8,128)(2,1)} async-done(((bf16[128,128]{1,0:T(8,128)(2,1)}), bf16[4096,128]{1,0:T(8,128)(2,1)}) %all-gather.7.cloned.1.call-update) | async-done | bytes 1048592 | tf_op jit(solution)/shard_map/all_gather | solution.py:71
  102.4 2.7 convolution_convert_fusion.6
  105.8 51.2 %all-gather.11.cloned.1.call-done = bf16[4096,1024]{1,0:T(8,128)(2,1)} async-done(((bf16[128,1024]{1,0:T(8,128)(2,1)}), bf16[4096,1024]{1,0:T(8,128)(2,1)}) %all-gather.11.cloned.1.call-update) | async-done | bytes 8388624 | tf_op jit(solution)/shard_map/all_gather | solution.py:66
  157.0 5.7 fusion.36
  162.8 40.4 %all-gather.15.cloned.1.call-done = bf16[8192,128]{1,0:T(8,128)(2,1)} async-done(((bf16[256,128]{1,0:T(8,128)(2,1)}), bf16[8192,128]{1,0:T(8,128)(2,1)}) %all-gather.15.cloned.1.call-update) | async-done | bytes 2097168 | tf_op jit(solution)/shard_map/all_gather | solution.py:92
  203.2 45.9 %all-gather.9.cloned.1.call-done = bf16[8192,128]{1,0:T(8,128)(2,1)} async-done(((bf16[256,128]{1,0:T(8,128)(2,1)}), bf16[8192,128]{1,0:T(8,128)(2,1)}) %all-gather.9.cloned.1.call-update) | async-done | bytes 2097168 | tf_op jit(solution)/shard_map/all_gather | solution.py:91
  249.2 19.2 %while.15 = (s32[]{:T(128)}, f32[256,8]{0,1:T(8,128)S(1)}, f32[256,8]{0,1:T(8,128)S(1)}, f32[256,8,128]{2,0,1:T(8,128)S(1)}, s32[8]{0:T(128)S(1)}, /*index=5*/s3...) while((s32[]{:T(128)}, f32[256,8]{0,1:T(8,128)S(1)}, ...), condition=%wide.region_6.7_spmd.clone, body=%wide.region_1.6_spmd.clone.sunk | while | flops 1101796608 | bytes 29503820 | solution.py:111
  250.7 8.7 %conditional.3 = ((f32[256,8]{0,1:T(8,128)S(1)}, f32[256,8]{0,1:T(8,128)S(1)}, f32[256,8,128]{2,0,1:T(8,128)S(1)})) conditional(s32[]{:T(128)} %convert_element_type.172, (f32[256,8]{0,1:T(8,128)S(1)}, f32[256,8]{0,1:T(8,128)S(1)}, f32[256,8,128]{2,0,1:T(8,128)S(1)}) %tuple.52, (s32[]{:T(128)}, s32[]{:T(128)}, bf16[8192,128]{1,0:T(8,128)(2,1)}, ...), branch_computations={%region_2.2_spmd, %region_3.5_spmd} | conditional | flops 1101796608 | bytes 29502546 | solution.py:101
  250.9 2.4 fusion.2
  255.4 3.9 fusion.8
  268.9 41.3 %all-gather.17.cloned.1.call-done = bf16[1024,4096]{1,0:T(8,128)(2,1)} async-done(((bf16[1024,128]{1,0:T(8,128)(2,1)}), bf16[1024,4096]{1,0:T(8,128)(2,1)}) %all-gather.17.cloned.1.call-update) | async-done | bytes 8388624 | tf_op jit(solution)/shard_map/all_gather | solution.py:116
  310.1 7.1 %convolution_convert_fusion.2 = bf16[256,4096]{1,0:T(8,128)(2,1)} fusion(bf16[256,1024]{0,1:T(8,128)(2,1)S(1)} %bitcast.55, bf16[1024,4096]{1,0:T(8,128)(2,1)} %all-gather.17.cloned.1.call-done), kind=kOutput, calls=%fused_computation.34 | convolution fusion | flops 2148532224 | bytes 11010048 | tf_op jit(solution)/shard_map/dot_general | solution.py:114
  317.9 76.3 %all-reduce.2.cloned.1.call-done = bf16[256,4096]{1,0:T(8,128)(2,1)} async-done(((bf16[256,4096]{1,0:T(8,128)(2,1)}), bf16[256,4096]{1,0:T(8,128)(2,1)}) %all-reduce.2.cloned.1.call-update) | async-done | bytes 2097168 | tf_op jit(solution)/shard_map/psum | solution.py:119
  394.2 3.2 fusion.24
  399.4 80.9 %all_to_all.10 = bf16[32,24,4096]{2,1,0:T(8,128)(2,1)S(1)} all-to-all(bf16[32,24,4096]{2,1,0:T(8,128)(2,1)S(1)} %bitcast.51), channel_id=1, replica_groups=mesh['grp'=4,'fsdp'=32] {'fsdp'}, dimensions={0} | all-to-all | bytes 12582912 | tf_op jit(solution)/shard_map/all_to_all | solution.py:149
  480.3 11.7 %fusion.21 = f32[768,1536]{1,0:T(8,128)} fusion(bf16[768,4096]{1,0:T(8,128)(2,1)S(1)} %bitcast.54, bf16[1,4096,1536]{2,1,0:T(8,128)(2,1)S(1)} %bitcast.57), kind=kOutput, calls=%fused_computation.24 | convolution fusion | flops 9663676416 | bytes 23592960 | tf_op jit(solution)/shard_map/dot_general | solution.py:152
  491.9 10.3 %convolution_convert_fusion.1 = bf16[768,4096]{1,0:T(8,128)(2,1)} fusion(bf16[1,768,4096]{2,1,0:T(8,128)(2,1)} %param.25, f32[768,1536]{1,0:T(8,128)} %fusion.21), kind=kOutput, calls=%fused_computation.27 | convolution fusion | flops 4838522880 | bytes 17301504 | tf_op jit(solution)/shard_map/dot_general | solution.py:154
  502.2 4.8 all-to-all-start.1
  507.2 77.7 %all-to-all-done.1 = bf16[32,24,4096]{2,1,0:T(8,128)(2,1)} async-done(((bf16[32,24,4096]{2,1,0:T(8,128)(2,1)}), bf16[32,24,4096]{2,1,0:T(8,128)(2,1)}, u32[]{:S(2)}, u32[]{:S(2)}) %all-to-all-start.1) | async-done | bytes 6291488 | tf_op jit(solution)/shard_map/all_to_all | solution.py:155
  584.9 6.1 convolution_convert_fusion.3
  591.0 34.6 %reduce-scatter.2.cloned.1.call-done = bf16[256,1024]{1,0:T(8,128)(2,1)} async-done(((bf16[256,4096]{1,0:T(8,128)(2,1)}), bf16[256,1024]{1,0:T(8,128)(2,1)}) %reduce-scatter.2.cloned.1.call-update) | async-done | bytes 524304 | tf_op jit(solution)/shard_map/reduce_scatter | solution.py:170
  627.6 3.1 copy.51
  (86 shorter events, 18.9 us)
Async XLA Ops:
  7.2 0.8 copy-start
  7.2 95.3 %copy-start.2 = (bf16[256,4096]{1,0:T(8,128)(2,1)S(1)}, bf16[256,4096]{1,0:T(8,128)(2,1)}, u32[]{:S(2)}) copy-start(bf16[256,4096]{1,0:T(8,128)(2,1)} %param.15) | copy-start | bytes 6291460
  7.2 95.3 %copy-start.6 = (f32[4096]{0:T(1024)S(1)}, f32[4096]{0:T(1024)}, u32[]{:S(2)}) copy-start(f32[4096]{0:T(1024)} %param.16) | copy-start | bytes 49156
  7.2 50.3 %all-gather.13.cloned.1.call-start = ((), (), s32[]{:S(2)}) async-start(), calls=%async_computation.6 | async-start | bytes 1081344 | tf_op jit(solution)/shard_map/all_gather | solution.py:76
  8.7 93.8 %all-gather.7.cloned.1.call-start = ((), (), s32[]{:S(2)}) async-start(), calls=%async_computation.3 | async-start | bytes 1081344 | tf_op jit(solution)/shard_map/all_gather | solution.py:71
  10.1 146.8 %all-gather.11.cloned.1.call-start = ((), (), s32[]{:S(2)}) async-start(), calls=%async_computation.5 | async-start | bytes 8650752 | tf_op jit(solution)/shard_map/all_gather | solution.py:66
  10.8 192.3 %all-gather.15.cloned.1.call-start = ((), (), s32[]{:S(2)}) async-start(), calls=%async_computation.7 | async-start | bytes 2162688 | tf_op jit(solution)/shard_map/all_gather | solution.py:92
  60.8 188.3 %all-gather.9.cloned.1.call-start = ((), (), s32[]{:S(2)}) async-start(), calls=%async_computation.4 | async-start | bytes 2162688 | tf_op jit(solution)/shard_map/all_gather | solution.py:91
  105.1 205.0 %all-gather.17.cloned.1.call-start = ((), (), s32[]{:S(2)}) async-start(), calls=%async_computation.8 | async-start | bytes 8650752 | tf_op jit(solution)/shard_map/all_gather | solution.py:116
  105.7 288.5 %all-reduce.2.cloned.1.call-start = ((), (), s32[]{:S(2)}) async-start(), calls=%async_computation.9 | async-start | bytes 4194304 | tf_op jit(solution)/shard_map/psum | solution.py:119
  310.1 7.2 %copy-start.3 = (s32[256,8]{0,1:T(8,128)S(1)}, s32[256,8]{0,1:T(8,128)}, u32[]{:S(2)}) copy-start(s32[256,8]{0,1:T(8,128)} %param.22) | copy-start | bytes 24580
  317.2 80.1 %copy-start.4 = (f32[4096]{0:T(1024)S(1)}, f32[4096]{0:T(1024)}, u32[]{:S(2)}) copy-start(f32[4096]{0:T(1024)} %param.17) | copy-start | bytes 49156
  397.4 82.9 %slice-start = ((s8[12582912]{0:T(1024)(128)(4,1)}), s8[4194304]{0:T(1024)(128)(4,1)S(1)}, s32[]{:S(2)}) async-start(s8[12582912]{0:T(1024)(128)(4,1)} %bitcast.56), calls=%async_computation.11 | async-start | bytes 8388608
  397.4 82.9 %slice-start.1 = ((s8[12582912]{0:T(1024)(128)(4,1)}), s8[4194304]{0:T(1024)(128)(4,1)S(1)}, s32[]{:S(2)}) async-start(s8[12582912]{0:T(1024)(128)(4,1)} %bitcast.56), calls=%async_computation.12 | async-start | bytes 8388608
  399.4 80.9 %slice-start.2 = ((s8[12582912]{0:T(1024)(128)(4,1)}), s8[4194304]{0:T(1024)(128)(4,1)S(1)}, s32[]{:S(2)}) async-start(s8[12582912]{0:T(1024)(128)(4,1)} %bitcast.56), calls=%async_computation.13 | async-start | bytes 8388608
  502.2 4.9 copy-start.5
  502.2 82.7 %all-to-all-start.1 = ((bf16[32,24,4096]{2,1,0:T(8,128)(2,1)}), bf16[32,24,4096]{2,1,0:T(8,128)(2,1)}, u32[]{:S(2)}, u32[]{:S(2)}) async-start(bf16[32,24,4096]{2,1,0:T(8,128)(2,1)} %bitcast.53), calls=%async_computation.1 | async-start | bytes 12582912 | tf_op jit(solution)/shard_map/all_to_all | solution.py:155
  507.0 118.5 %reduce-scatter.2.cloned.1.call-start = ((), (), s32[]{:S(2)}) async-start(), calls=%async_computation.10 | async-start | bytes 2621440 | tf_op jit(solution)/shard_map/reduce_scatter | solution.py:170
  584.9 45.9 %copy-start.1 = (bf16[128,256]{1,0:T(8,128)(2,1)S(1)}, bf16[128,256]{1,0:T(8,128)(2,1)}, u32[]{:S(2)}) copy-start(bf16[128,256]{1,0:T(8,128)(2,1)} %param.20) | copy-start | bytes 196612
Sparse Core Ops, SparseCore 0:
  10.9 46.5 all-gather.12
  60.3 42.0 all-gather.6
  104.7 52.1 all-gather.10
  159.6 43.4 all-gather.14
  205.9 43.2 all-gather.8
  251.2 58.9 all-gather.16
  317.4 76.7 all-reduce.1
  591.1 34.4 reduce-scatter.1
where the time goes:
time: 639 us; the launch traced here: 638 us
  waiting for transfers between devices  455 us (71%)
  blocking collectives  80.9 us (13%)
  matrix products  55.6 us (9%)
  between operations  14.4 us (2%)
  local copies, waits for them, and re-layouts  11.1 us (2%)
  other arithmetic  9.87 us (2%)
    all_to_all x1, blocking collectives, on_device(): lax.all_to_all(outbound, 'fsdp', split_axis=0, concat_axis=0, tiled=True)  80.9 us
    all_to_all x1, waiting for transfers between devices, on_device(): lax.all_to_all(result.reshape(fsdp_size, slot_count, model_width), 'fsdp'...  77.7 us
    psum x1, waiting for transfers between devices, on_device(): lax.psum(head_part.astype(jnp.float32).astype(jnp.bfloat16), 'grp')  76.3 us
    all_gather x1, waiting for transfers between devices, on_device(): lax.all_gather(w_query, 'fsdp', axis=0, tiled=True)  51.2 us
    all_gather x1, waiting for transfers between devices, on_device(): key_rows = lax.all_gather(key_local, 'fsdp', axis=0, tiled=True)  45.9 us
    all_gather x1, waiting for transfers between devices, on_device(): lax.all_gather(value_cols, 'fsdp', axis=0, tiled=True)  44.5 us
    all_gather x1, waiting for transfers between devices, on_device(): lax.all_gather(key_cols, 'fsdp', axis=0, tiled=True)  41.6 us
    all_gather x1, waiting for transfers between devices, on_device(): lax.all_gather(w_out, 'fsdp', axis=1, tiled=True)  41.3 us
  transfers between devices with their start and end apart: 9, of which 9 were waited for; matrix products, arithmetic and copies ran while one was open for 5% of the time, Pallas kernels for 0%

commit v1 on v0

--- a/solution.py
+++ b/solution.py
@@ -1,3 +1,4 @@
+import functools
 import jax
 import jax.numpy as jnp
 from jax import lax
@@ -8,6 +9,13 @@
 FFW = 768
 EPSILON = 1e-06
 FLOOR_SCORE = -1e30
+
+
+def settle_files(target, lane_axis):
+    return lax.all_gather(target, lane_axis).sum(axis=0)
+
+
+fix_the_area = functools.partial(settle_files, lane_axis="grp")
 
 
 def rms_scale(row_data, gain):
@@ -116,7 +124,7 @@
         lax.all_gather(w_out, "fsdp", axis=1, tiled=True),
         preferred_element_type=jnp.float32,
     ).astype(jnp.bfloat16)
-    attn_branch = lax.psum(head_part.astype(jnp.float32).astype(jnp.bfloat16), "grp")
+    attn_branch = fix_the_area(head_part.astype(jnp.float32).astype(jnp.bfloat16))
     resid = (tokens.astype(jnp.float32) + attn_branch.astype(jnp.float32)).astype(jnp.bfloat16)
     ffn_in = rms_scale(resid, ffn_gain)
     top_count = routes.shape[1]

time: 639 us -> 668 us (1.045)
  waiting for transfers between devices: 455 us -> 480 us
  other arithmetic: 9.87 us -> 16.8 us
    all_gather x0 -> x1, waiting for transfers between devices: none -> 101 us  [settle_files(): return lax.all_gather(target, lane_axis).sum(axis=0)]
    psum x1 -> x0, waiting for transfers between devices: 76.3 us -> none  [on_device(): lax.psum(head_part.astype(jnp.float32).astype(jnp.bfloat16), 'grp')]
    reduce_sum x0 -> x1, other arithmetic: none -> 6.89 us  [settle_files(): return lax.all_gather(target, lane_axis).sum(axis=0)]
  transfers between devices with their start and end apart: 9 -> 9, of which waited for: 9 -> 9; matrix products, arithmetic and copies ran while one was open for 5% -> 4% of each run, Pallas kernels for 0% -> 0%
where the time goes in v1:
time: 668 us; the launch traced here: 667 us
  waiting for transfers between devices  480 us (72%)
  blocking collectives  80.9 us (12%)
  matrix products  55.8 us (8%)
  other arithmetic  16.8 us (3%)
  between operations  14.4 us (2%)
  local copies, waits for them, and re-layouts  8.01 us (1%)
    all_gather x1, waiting for transfers between devices, settle_files(): return lax.all_gather(target, lane_axis).sum(axis=0)  101 us
    all_to_all x1, blocking collectives, on_device(): lax.all_to_all(outbound, 'fsdp', split_axis=0, concat_axis=0, tiled=True)  80.9 us
    all_to_all x1, waiting for transfers between devices, on_device(): lax.all_to_all(result.reshape(fsdp_size, slot_count, model_width), 'fsdp'...  77.7 us
    all_gather x1, waiting for transfers between devices, on_device(): lax.all_gather(w_query, 'fsdp', axis=0, tiled=True)  51.2 us
    all_gather x1, waiting for transfers between devices, on_device(): value_rows = lax.all_gather(value_local, 'fsdp', axis=0, tiled=True)  45.9 us
    all_gather x1, waiting for transfers between devices, on_device(): lax.all_gather(key_cols, 'fsdp', axis=0, tiled=True)  44.5 us
    all_gather x1, waiting for transfers between devices, on_device(): lax.all_gather(value_cols, 'fsdp', axis=0, tiled=True)  41.6 us
    all_gather x1, waiting for transfers between devices, on_device(): lax.all_gather(w_out, 'fsdp', axis=1, tiled=True)  41.2 us
  transfers between devices with their start and end apart: 9, of which 9 were waited for; matrix products, arithmetic and copies ran while one was open for 4% of the time, Pallas kernels for 0%

profile of v1, /device:TPU:1, one launch (start us, length us, event | category | flops | bytes accessed | tf_op | source)
XLA Modules:
  0.0 667.0 jit_solution(4176876372559982364)
XLA Ops:
  13.0 44.5 %all-gather.9.cloned.1.call-done = bf16[4096,128]{1,0:T(8,128)(2,1)} async-done(((bf16[128,128]{1,0:T(8,128)(2,1)}), bf16[4096,128]{1,0:T(8,128)(2,1)}) %all-gather.9.cloned.1.call-update) | async-done | bytes 1048592 | tf_op jit(solution)/shard_map/all_gather | solution.py:79
  57.5 3.3 convolution_convert_fusion.6
  60.9 41.6 %all-gather.15.cloned.1.call-done = bf16[4096,128]{1,0:T(8,128)(2,1)} async-done(((bf16[128,128]{1,0:T(8,128)(2,1)}), bf16[4096,128]{1,0:T(8,128)(2,1)}) %all-gather.15.cloned.1.call-update) | async-done | bytes 1048592 | tf_op jit(solution)/shard_map/all_gather | solution.py:84
  102.4 2.7 convolution_convert_fusion.5
  105.8 51.2 %all-gather.13.cloned.1.call-done = bf16[4096,1024]{1,0:T(8,128)(2,1)} async-done(((bf16[128,1024]{1,0:T(8,128)(2,1)}), bf16[4096,1024]{1,0:T(8,128)(2,1)}) %all-gather.13.cloned.1.call-update) | async-done | bytes 8388624 | tf_op jit(solution)/shard_map/all_gather | solution.py:74
  157.0 5.7 fusion.36
  162.8 40.4 %all-gather.11.cloned.1.call-done = bf16[8192,128]{1,0:T(8,128)(2,1)} async-done(((bf16[256,128]{1,0:T(8,128)(2,1)}), bf16[8192,128]{1,0:T(8,128)(2,1)}) %all-gather.11.cloned.1.call-update) | async-done | bytes 2097168 | tf_op jit(solution)/shard_map/all_gather | solution.py:99
  203.2 45.9 %all-gather.17.cloned.1.call-done = bf16[8192,128]{1,0:T(8,128)(2,1)} async-done(((bf16[256,128]{1,0:T(8,128)(2,1)}), bf16[8192,128]{1,0:T(8,128)(2,1)}) %all-gather.17.cloned.1.call-update) | async-done | bytes 2097168 | tf_op jit(solution)/shard_map/all_gather | solution.py:100
  249.2 19.2 %while.15 = (s32[]{:T(128)}, f32[256,8]{0,1:T(8,128)S(1)}, f32[256,8]{0,1:T(8,128)S(1)}, f32[256,8,128]{2,0,1:T(8,128)S(1)}, s32[8]{0:T(128)S(1)}, /*index=5*/s3...) while((s32[]{:T(128)}, f32[256,8]{0,1:T(8,128)S(1)}, ...), condition=%wide.region_6.7_spmd.clone, body=%wide.region_1.6_spmd.clone.sunk | while | flops 1101796608 | bytes 29503820 | solution.py:119
  250.5 8.7 %conditional.3 = ((f32[256,8]{0,1:T(8,128)S(1)}, f32[256,8]{0,1:T(8,128)S(1)}, f32[256,8,128]{2,0,1:T(8,128)S(1)})) conditional(s32[]{:T(128)} %convert_element_type.174, (f32[256,8]{0,1:T(8,128)S(1)}, f32[256,8]{0,1:T(8,128)S(1)}, f32[256,8,128]{2,0,1:T(8,128)S(1)}) %tuple.52, (s32[]{:T(128)}, s32[]{:T(128)}, bf16[8192,128]{1,0:T(8,128)(2,1)}, ...), branch_computations={%region_2.2_spmd, %region_3.5_spmd} | conditional | flops 1101796608 | bytes 29502546 | solution.py:109
  250.7 2.4 fusion.2
  255.2 3.9 fusion.8
  268.9 41.2 %all-gather.19.cloned.1.call-done = bf16[1024,4096]{1,0:T(8,128)(2,1)} async-done(((bf16[1024,128]{1,0:T(8,128)(2,1)}), bf16[1024,4096]{1,0:T(8,128)(2,1)}) %all-gather.19.cloned.1.call-update) | async-done | bytes 8388624 | tf_op jit(solution)/shard_map/all_gather | solution.py:124
  310.1 7.1 %convolution_convert_fusion.2 = bf16[256,4096]{1,0:T(8,128)(2,1)} fusion(bf16[256,1024]{0,1:T(8,128)(2,1)S(1)} %bitcast.57, bf16[1024,4096]{1,0:T(8,128)(2,1)} %all-gather.19.cloned.1.call-done), kind=kOutput, calls=%fused_computation.34 | convolution fusion | flops 2148532224 | bytes 11010048 | tf_op jit(solution)/shard_map/dot_general | solution.py:122
  317.9 100.7 %all-gather.21.cloned.1.call-done = bf16[1024,4096]{1,0:T(8,128)(2,1)} async-done(((bf16[256,4096]{1,0:T(8,128)(2,1)}), bf16[1024,4096]{1,0:T(8,128)(2,1)}) %all-gather.21.cloned.1.call-update) | async-done | bytes 8388624 | tf_op jit(solution)/shard_map/all_gather | solution.py:15
  418.6 6.9 %reduce_sum.55 = bf16[256,4096]{1,0:T(8,128)(2,1)} reduce(bf16[4,256,4096]{2,1,0:T(8,128)(2,1)} %bitcast.54, bf16[]{:T(256)} %constant.115.clone.1), dimensions={0}, to_apply=%region_7.8 | reduce | flops 3145728 | bytes 10485762 | tf_op jit(solution)/shard_map/reduce_sum | solution.py:15
  425.4 3.2 fusion.24
  430.7 80.9 %all_to_all.10 = bf16[32,24,4096]{2,1,0:T(8,128)(2,1)S(1)} all-to-all(bf16[32,24,4096]{2,1,0:T(8,128)(2,1)S(1)} %bitcast.52), channel_id=1, replica_groups=mesh['grp'=4,'fsdp'=32] {'fsdp'}, dimensions={0} | all-to-all | bytes 12582912 | tf_op jit(solution)/shard_map/all_to_all | solution.py:157
  511.5 11.7 %fusion.21 = f32[768,1536]{1,0:T(8,128)} fusion(bf16[768,4096]{1,0:T(8,128)(2,1)S(1)} %bitcast.56, bf16[1,4096,1536]{2,1,0:T(8,128)(2,1)S(1)} %bitcast.59), kind=kOutput, calls=%fused_computation.24 | convolution fusion | flops 9663676416 | bytes 23592960 | tf_op jit(solution)/shard_map/dot_general | solution.py:160
  523.2 10.4 %convolution_convert_fusion.1 = bf16[768,4096]{1,0:T(8,128)(2,1)} fusion(bf16[1,768,4096]{2,1,0:T(8,128)(2,1)} %param.25, f32[768,1536]{1,0:T(8,128)} %fusion.21), kind=kOutput, calls=%fused_computation.27 | convolution fusion | flops 4838522880 | bytes 17301504 | tf_op jit(solution)/shard_map/dot_general | solution.py:162
  533.6 4.8 all-to-all-start.1
  538.5 77.7 %all-to-all-done.1 = bf16[32,24,4096]{2,1,0:T(8,128)(2,1)} async-done(((bf16[32,24,4096]{2,1,0:T(8,128)(2,1)}), bf16[32,24,4096]{2,1,0:T(8,128)(2,1)}, u32[]{:S(2)}, u32[]{:S(2)}) %all-to-all-start.1) | async-done | bytes 6291488 | tf_op jit(solution)/shard_map/all_to_all | solution.py:163
  616.2 6.1 convolution_convert_fusion.3
  622.4 35.7 %reduce-scatter.2.cloned.1.call-done = bf16[256,1024]{1,0:T(8,128)(2,1)} async-done(((bf16[256,4096]{1,0:T(8,128)(2,1)}), bf16[256,1024]{1,0:T(8,128)(2,1)}) %reduce-scatter.2.cloned.1.call-update) | async-done | bytes 524304 | tf_op jit(solution)/shard_map/reduce_scatter | solution.py:178
  (86 shorter events, 18.9 us)
Async XLA Ops:
  7.2 0.8 copy-start
  7.2 95.3 %copy-start.2 = (bf16[256,4096]{1,0:T(8,128)(2,1)S(1)}, bf16[256,4096]{1,0:T(8,128)(2,1)}, u32[]{:S(2)}) copy-start(bf16[256,4096]{1,0:T(8,128)(2,1)} %param.15) | copy-start | bytes 6291460
  7.2 95.3 %copy-start.6 = (f32[4096]{0:T(1024)S(1)}, f32[4096]{0:T(1024)}, u32[]{:S(2)}) copy-start(f32[4096]{0:T(1024)} %param.16) | copy-start | bytes 49156
  7.2 50.3 %all-gather.9.cloned.1.call-start = ((), (), s32[]{:S(2)}) async-start(), calls=%async_computation.3 | async-start | bytes 1081344 | tf_op jit(solution)/shard_map/all_gather | solution.py:79
  8.7 93.8 %all-gather.15.cloned.1.call-start = ((), (), s32[]{:S(2)}) async-start(), calls=%async_computation.6 | async-start | bytes 1081344 | tf_op jit(solution)/shard_map/all_gather | solution.py:84
  10.1 146.8 %all-gather.13.cloned.1.call-start = ((), (), s32[]{:S(2)}) async-start(), calls=%async_computation.5 | async-start | bytes 8650752 | tf_op jit(solution)/shard_map/all_gather | solution.py:74
  10.8 192.3 %all-gather.11.cloned.1.call-start = ((), (), s32[]{:S(2)}) async-start(), calls=%async_computation.4 | async-start | bytes 2162688 | tf_op jit(solution)/shard_map/all_gather | solution.py:99
  60.8 188.3 %all-gather.17.cloned.1.call-start = ((), (), s32[]{:S(2)}) async-start(), calls=%async_computation.7 | async-start | bytes 2162688 | tf_op jit(solution)/shard_map/all_gather | solution.py:100
  105.1 205.0 %all-gather.19.cloned.1.call-start = ((), (), s32[]{:S(2)}) async-start(), calls=%async_computation.8 | async-start | bytes 8650752 | tf_op jit(solution)/shard_map/all_gather | solution.py:124
  105.7 312.8 %all-gather.21.cloned.1.call-start = ((), (), s32[]{:S(2)}) async-start(), calls=%async_computation.10 | async-start | bytes 10485760 | tf_op jit(solution)/shard_map/all_gather | solution.py:15
  310.1 7.2 %copy-start.3 = (s32[256,8]{0,1:T(8,128)S(1)}, s32[256,8]{0,1:T(8,128)}, u32[]{:S(2)}) copy-start(s32[256,8]{0,1:T(8,128)} %param.22) | copy-start | bytes 24580
  425.4 3.2 copy-start.4
  428.7 82.9 %slice-start = ((s8[12582912]{0:T(1024)(128)(4,1)}), s8[4194304]{0:T(1024)(128)(4,1)S(1)}, s32[]{:S(2)}) async-start(s8[12582912]{0:T(1024)(128)(4,1)} %bitcast.58), calls=%async_computation.11 | async-start | bytes 8388608
  428.7 82.9 %slice-start.1 = ((s8[12582912]{0:T(1024)(128)(4,1)}), s8[4194304]{0:T(1024)(128)(4,1)S(1)}, s32[]{:S(2)}) async-start(s8[12582912]{0:T(1024)(128)(4,1)} %bitcast.58), calls=%async_computation.12 | async-start | bytes 8388608
  430.7 80.9 %slice-start.2 = ((s8[12582912]{0:T(1024)(128)(4,1)}), s8[4194304]{0:T(1024)(128)(4,1)S(1)}, s32[]{:S(2)}) async-start(s8[12582912]{0:T(1024)(128)(4,1)} %bitcast.58), calls=%async_computation.13 | async-start | bytes 8388608
  533.6 4.9 copy-start.5
  533.6 82.7 %all-to-all-start.1 = ((bf16[32,24,4096]{2,1,0:T(8,128)(2,1)}), bf16[32,24,4096]{2,1,0:T(8,128)(2,1)}, u32[]{:S(2)}, u32[]{:S(2)}) async-start(bf16[32,24,4096]{2,1,0:T(8,128)(2,1)} %bitcast.55), calls=%async_computation.1 | async-start | bytes 12582912 | tf_op jit(solution)/shard_map/all_to_all | solution.py:163
  538.4 119.7 %reduce-scatter.2.cloned.1.call-start = ((), (), s32[]{:S(2)}) async-start(), calls=%async_computation.9 | async-start | bytes 2621440 | tf_op jit(solution)/shard_map/reduce_scatter | solution.py:178
  616.2 43.9 %copy-start.1 = (bf16[128,256]{1,0:T(8,128)(2,1)S(1)}, bf16[128,256]{1,0:T(8,128)(2,1)}, u32[]{:S(2)}) copy-start(bf16[128,256]{1,0:T(8,128)(2,1)} %param.19) | copy-start | bytes 196612
Sparse Core Ops, SparseCore 0:
  10.9 46.5 all-gather.8
  60.3 42.0 all-gather.14
  104.7 52.1 all-gather.12
  159.6 43.4 all-gather.10
  205.9 43.2 all-gather.16
  251.2 58.9 all-gather.18
  317.4 101.1 all-gather.20
  622.5 35.5 reduce-scatter.1
